TPU v7x, 32 devices: a whole 2x2x4 slice. The times are simulated.
32 devices in a mesh: gx: 8 (over z, y), gy: 4 (over x, core).
Axes of the slice: x: 2, y: 2, z: 4, core: 2. Of those that a mesh axis runs over, the one named last changes fastest.
Arguments:
- cell_means: float32 [30, 32, 16, 128], P(None, 'gx', 'gy'), may hold values from 0 to 1
- diffusion: float32 [32, 16, 128], P('gx', 'gy'), may hold values from 0.02 to 0.15
- mix_rate: float32 [32, 16, 128], P('gx', 'gy'), may hold values from 0.05 to 3
- send_lists: int32 [32, 32, 128], P(('gx', 'gy')), may hold values from 0 to 2047
- compositions: float32 [30, 131072], P(None, ('gx', 'gy')), may hold values from 0 to 1
- weights: float32 [131072], P(('gx', 'gy')), may hold values from 0.5 to 2
- particle_slots: int32 [131072], P(('gx', 'gy')), may hold values from 0 to 4095
- partners: int32 [131072], P(('gx', 'gy')), may hold values from 0 to 4095
Outputs:
- new_means: float32 [30, 32, 16, 128], P(None, 'gx', 'gy')
- new_compositions: float32 [30, 131072], P(None, ('gx', 'gy'))
Inputs may be any that keep to these rules, and one draw needn't show every extreme that they name: particle_slots = s * 128 + r names slot r of the list that tile s sends to the particle's device.
All inputs are finite; a program needn't handle non-finite values.
Results may differ from a plain program's by a relative error of at most 0.00002.
Values sent between devices are 32-bit elements; how exact they have to be, the bound alone decides.
A program may use at most 64 MiB of HBM per device.

v0:
```python
import jax
import jax.numpy as jnp
from jax import lax
from jax.sharding import PartitionSpec as P

PAIR_RATE = 0.3


def with_halo(shard, sides, width):
    for axis, dim in sides:
        devices, length = (lax.axis_size(axis), shard.shape[dim])
        up = [(i, (i + 1) % devices) for i in range(devices - 1)]
        down = [(j, i) for i, j in up]
        last = lax.slice_in_dim(shard, length - width, length, axis=dim)
        initial = lax.slice_in_dim(shard, 0, width, axis=dim)
        before = lax.ppermute(last, axis, up)
        after = lax.ppermute(initial, axis, down)
        shard = jnp.concatenate([before, shard, after], axis=dim)
    return shard


def on_device(
    cell_means, diffusion, mix_rate, send_lists, compositions, weights, particle_slots, partners
):
    species, rows_x, rows_y, depth = cell_means.shape
    cell_count = rows_x * rows_y * depth
    groups_x = lax.axis_size("gx")
    groups_y = lax.axis_size("gy")
    padded = with_halo(cell_means, (("gx", 1), ("gy", 2)), 1)
    deepened = jnp.pad(cell_means, ((0, 0), (0, 0), (0, 0), (1, 1)))
    neighbours = (
        padded[:, 2:, 1:-1] + padded[:, :-2, 1:-1] + padded[:, 1:-1, 2:] + padded[:, 1:-1, :-2]
    )
    neighbours = neighbours + deepened[:, :, :, 2:] + deepened[:, :, :, :-2]
    filtered = cell_means + diffusion[None] * (neighbours - 6.0 * cell_means)
    fields = jnp.concatenate(
        [filtered.reshape(species, cell_count), mix_rate.reshape(1, cell_count)], 0
    )
    slots_peer = send_lists.shape[2]
    slot_count = groups_x * groups_y * slots_peer
    flat_list = send_lists[0].reshape(-1)
    outgoing = jnp.take(fields, flat_list, axis=1)
    received = lax.all_to_all(outgoing, ("gx", "gy"), split_axis=1, concat_axis=1, tiled=True)
    local_means = jnp.take(received, particle_slots, axis=1)
    mates = jnp.take(compositions, partners, axis=1)
    blend_rate = 1.0 - jnp.exp(-local_means[species])
    new_compositions = (
        compositions
        - blend_rate[None] * (compositions - local_means[:species])
        - PAIR_RATE * (compositions - mates)
    )
    weighted = jnp.concatenate([weights[None] * new_compositions, weights[None]], 0)
    moments = jnp.zeros((species + 1, slot_count), jnp.float32).at[:, particle_slots].add(weighted)
    returned = lax.all_to_all(moments, ("gx", "gy"), split_axis=1, concat_axis=1, tiled=True)
    totals = jnp.zeros((species + 1, cell_count), jnp.float32).at[:, flat_list].add(returned)
    updated = (totals[:species] + fields[:species]) / (totals[species][None] + 1.0)
    return (updated.reshape(species, rows_x, rows_y, depth), new_compositions)


def solution(mesh):
    in_specs = (
        P(None, "gx", "gy", None),
        P("gx", "gy", None),
        P("gx", "gy", None),
        P(("gx", "gy"), None, None),
        P(None, ("gx", "gy")),
        P(("gx", "gy")),
        P(("gx", "gy")),
        P(("gx", "gy")),
    )
    out_specs = (P(None, "gx", "gy", None), P(None, ("gx", "gy")))
    return jax.shard_map(
        on_device, mesh=mesh, in_specs=in_specs, out_specs=out_specs, check_vma=False
    )
```

profile of v0, /device:TPU:0, one launch (start us, length us, event | category | flops | bytes accessed | tf_op | source)
XLA Modules:
  0.0 158.9 jit_solution(12772471050581777557)
XLA Ops:
  0.7 0.9 fusion.23
  1.6 4.9 %collective-permute-start.1 = (f32[30,1,4,128]{3,2,1,0:T(4,128)S(1)}, f32[30,1,4,128]{3,2,1,0:T(4,128)S(1)}, u32[]{:S(2)}, u32[]{:S(2)}) collective-permute-start(f32[30,1,4,128]{3,2,1,0:T(4,128)S(1)} %get-tuple-element.19), channel_id=1, source_target_pairs={{0,4},{4,8},{8,12},{12,16},{16,20},{20,24},{24,28},{1,5},{5,9},{9,... | collective-permute-start | bytes 184328 | tf_op jit(solution)/shard_map/ppermute | solution.py:16
  6.4 1.3 collective-permute-start
  7.7 0.7 compare_select_fusion
  8.5 1.0 constant_dynamic-update-slice_fusion.1
  9.5 3.0 %collective-permute-done = f32[30,1,4,128]{3,2,1,0:T(4,128)S(1)} collective-permute-done((f32[30,1,4,128]{3,2,1,0:T(4,128)S(1)}, f32[30,1,4,128]{3,2,1,0:T(4,128)S(1)}, u32[]{:S(2)}, u32[]{:S(2)}) %collective-permute-start) | collective-permute-done | bytes 61472 | tf_op jit(solution)/shard_map/ppermute | solution.py:17
  12.7 1.3 collective-permute-start.3
  14.0 1.3 collective-permute-start.2
  15.3 0.7 compare_and_fusion.1
  16.1 1.1 copy.72
  17.1 1.8 %collective-permute-done.2 = f32[30,6,1,128]{3,2,1,0:T(1,128)S(1)} collective-permute-done((f32[30,6,1,128]{3,2,1,0:T(1,128)S(1)}, f32[30,6,1,128]{3,2,1,0:T(1,128)S(1)}, u32[]{:S(2)}, u32[]{:S(2)}) %collective-permute-start.2) | collective-permute-done | bytes 92192 | tf_op jit(solution)/shard_map/ppermute | solution.py:17
  19.0 0.4 fusion.14
  19.4 0.4 copy.71
  20.1 14.2 %gather_fusion = f32[4096,31]{1,0:T(8,128)} fusion(f32[31,2048]{0,1:T(8,128)S(1)} %pad_maximum_fusion, s32[4096]{0:T(1024)S(1)} %broadcast_clamp_fusion.1), kind=kCustom, calls=%fused_computation | custom fusion | bytes 1032192 | tf_op jit(solution)/shard_map/jit(_take)/gather | solution.py:42
  34.3 2.2 %copy.73 = f32[31,32,128]{2,0,1:T(8,128)S(1)} copy(f32[31,32,128]{0,2,1:T(8,128)} %bitcast.37) | data formatting | bytes 1015808 | tf_op jit(solution)/shard_map/jit(_take)/gather | solution.py:42
  36.5 0.9 broadcast_select_fusion
  37.4 7.7 %all-to-all-start = ((f32[31,32,128]{2,0,1:T(8,128)}), f32[31,32,128]{2,0,1:T(8,128)}, u32[]{:S(2)}, u32[]{:S(2)}) async-start(f32[31,32,128]{2,0,1:T(8,128)} %broadcast_select_fusion), calls=%async_computation | async-start | bytes 1048576 | tf_op jit(solution)/shard_map/all_to_all | solution.py:43
  45.1 1.7 %copy.76 = f32[30,4096]{0,1:T(8,128)S(1)} copy(f32[30,4096]{1,0:T(8,128)} %param.12) | data formatting | bytes 983040 | tf_op args[4]
  46.8 14.2 %gather_fusion.2 = f32[4096,30]{1,0:T(8,128)} fusion(f32[30,4096]{0,1:T(8,128)S(1)} %copy.76, s32[4096]{0:T(1024)S(1)} %fusion.20), kind=kCustom, calls=%fused_computation.2 | custom fusion | bytes 999424 | tf_op jit(solution)/shard_map/jit(_take)/gather | solution.py:45
  61.0 3.0 %copy.77 = f32[4096,30]{0,1:T(8,128)} copy(f32[4096,30]{1,0:T(8,128)} %gather_fusion.2) | data formatting | bytes 983040 | tf_op jit(solution)/shard_map/jit(_take)/gather | solution.py:45
  64.1 1.7 %copy.74 = f32[31,32,128]{0,2,1:T(8,128)S(1)} copy(f32[31,32,128]{2,0,1:T(8,128)} %all-to-all-done) | data formatting | bytes 1015808 | tf_op jit(solution)/shard_map/all_to_all | solution.py:43
  65.7 14.2 %gather_fusion.1 = f32[4096,31]{1,0:T(8,128)} fusion(f32[31,4096]{0,1:T(8,128)S(1)} %bitcast.33, s32[4096]{0:T(1024)S(1)} %get-tuple-element.20), kind=kCustom, calls=%fused_computation.1 | custom fusion | bytes 1032192 | tf_op jit(solution)/shard_map/jit(_take)/gather | solution.py:44
  79.9 2.3 %copy.75 = f32[4096,31]{0,1:T(8,128)S(1)} copy(f32[4096,31]{1,0:T(8,128)} %gather_fusion.1) | data formatting | bytes 1015808 | tf_op jit(solution)/shard_map/jit(_take)/gather | solution.py:44
  82.4 0.9 broadcast_multiply_fusion
  83.3 2.0 %copy.78 = f32[4096,31]{1,0:T(8,128)} copy(f32[4096,31]{0,1:T(8,128)S(1)} %maximum_bitcast_fusion) | data formatting | bytes 1015808 | tf_op jit(solution)/shard_map/concatenate | solution.py:52
  85.4 23.2 %scatter_custom_fusion = f32[31,4096]{0,1:T(8,128)S(1)} fusion(s32[4096]{0:T(1024)S(1)} %get-tuple-element.21, f32[4096,31]{1,0:T(8,128)} %copy.78, f32[]{:T(128)} %constant.25.clone.1), kind=kCustom, calls=%fused_computation.10 | custom fusion | flops 126976 | bytes 508416 | tf_op jit(solution)/shard_map/scatter-add | solution.py:53
  108.5 1.4 copy.79
  110.0 21.3 %all_to_all.21 = f32[31,32,128]{2,0,1:T(8,128)S(1)} all-to-all(f32[31,32,128]{2,0,1:T(8,128)} %copy.79), channel_id=1, replica_groups=mesh['gx'=8,'gy'=4] {'gx','gy'}, dimensions={1} | all-to-all | bytes 1015808 | tf_op jit(solution)/shard_map/all_to_all | solution.py:54
  131.9 2.0 %copy.81 = f32[4096,31]{1,0:T(8,128)} copy(f32[4096,31]{0,1:T(8,128)S(1)} %bitcast.38) | data formatting | bytes 1015808 | tf_op jit(solution)/shard_map/all_to_all | solution.py:54
  133.9 22.9 %scatter_custom_fusion.1 = f32[31,2048]{0,1:T(8,128)S(1)} fusion(s32[4096]{0:T(1024)S(1)} %bitcast.42, f32[4096,31]{1,0:T(8,128)} %copy.81, f32[]{:T(128)} %constant.25.clone.1), kind=kCustom, calls=%fused_computation.22 | custom fusion | flops 126976 | bytes 254464 | tf_op jit(solution)/shard_map/scatter-add | solution.py:55
  156.8 0.6 fusion
  157.8 1.0 copy.82
  (33 shorter events, 1.7 us)
Async XLA Ops:
  0.6 18.3 %copy-start.2 = (f32[30,4,4,128]{3,2,1,0:T(4,128)S(1)}, f32[30,4,4,128]{3,2,1,0:T(4,128)}, u32[]{:S(2)}) copy-start(f32[30,4,4,128]{3,2,1,0:T(4,128)} %param.8) | copy-start | bytes 737284
  0.6 18.3 %copy-start.6 = (f32[4,4,128]{2,1,0:T(4,128)S(1)}, f32[4,4,128]{2,1,0:T(4,128)}, u32[]{:S(2)}) copy-start(f32[4,4,128]{2,1,0:T(4,128)} %param.9) | copy-start | bytes 24580
  1.6 6.9 %collective-permute-start.1 = (f32[30,1,4,128]{3,2,1,0:T(4,128)S(1)}, f32[30,1,4,128]{3,2,1,0:T(4,128)S(1)}, u32[]{:S(2)}, u32[]{:S(2)}) collective-permute-start(f32[30,1,4,128]{3,2,1,0:T(4,128)S(1)} %get-tuple-element.19), channel_id=1, source_target_pairs={{0,4},{4,8},{8,12},{12,16},{16,20},{20,24},{24,28},{1,5},{5,9},{9,... | collective-permute-start | bytes 184328 | tf_op jit(solution)/shard_map/ppermute | solution.py:16
  6.4 6.1 %collective-permute-start = (f32[30,1,4,128]{3,2,1,0:T(4,128)S(1)}, f32[30,1,4,128]{3,2,1,0:T(4,128)S(1)}, u32[]{:S(2)}, u32[]{:S(2)}) collective-permute-start(f32[30,1,4,128]{3,2,1,0:T(4,128)S(1)} %get-tuple-element.18), channel_id=1, source_target_pairs={{4,0},{8,4},{12,8},{16,12},{20,16},{24,20},{28,24},{5,1},{9,5},{13... | collective-permute-start | bytes 184328 | tf_op jit(solution)/shard_map/ppermute | solution.py:17
  12.7 4.4 %collective-permute-start.3 = (f32[30,6,1,128]{3,2,1,0:T(1,128)S(1)}, f32[30,6,1,128]{3,2,1,0:T(1,128)S(1)}, u32[]{:S(2)}, u32[]{:S(2)}) collective-permute-start(f32[30,6,1,128]{3,2,1,0:T(1,128)S(1)} %get-tuple-element.17), channel_id=1, source_target_pairs={{0,1},{1,2},{2,3},{4,5},{5,6},{6,7},{8,9},{9,10},{10,11},{12,13},{... | collective-permute-start | bytes 276488 | tf_op jit(solution)/shard_map/ppermute | solution.py:16
  14.0 4.9 %collective-permute-start.2 = (f32[30,6,1,128]{3,2,1,0:T(1,128)S(1)}, f32[30,6,1,128]{3,2,1,0:T(1,128)S(1)}, u32[]{:S(2)}, u32[]{:S(2)}) collective-permute-start(f32[30,6,1,128]{3,2,1,0:T(1,128)S(1)} %get-tuple-element.16), channel_id=1, source_target_pairs={{1,0},{2,1},{3,2},{5,4},{6,5},{7,6},{9,8},{10,9},{11,10},{13,12},{... | collective-permute-start | bytes 276488 | tf_op jit(solution)/shard_map/ppermute | solution.py:17
  37.4 9.4 %copy-start.4 = (s32[4096]{0:T(1024)S(1)}, s32[4096]{0:T(1024)}, u32[]{:S(2)}) copy-start(s32[4096]{0:T(1024)} %param.15) | copy-start | bytes 49156
  37.4 26.7 %all-to-all-start = ((f32[31,32,128]{2,0,1:T(8,128)}), f32[31,32,128]{2,0,1:T(8,128)}, u32[]{:S(2)}, u32[]{:S(2)}) async-start(f32[31,32,128]{2,0,1:T(8,128)} %broadcast_select_fusion), calls=%async_computation | async-start | bytes 1048576 | tf_op jit(solution)/shard_map/all_to_all | solution.py:43
  61.0 3.0 %copy-start.3 = (s32[4096]{0:T(1024)S(1)}, s32[4096]{0:T(1024)}, u32[]{:S(2)}) copy-start(s32[4096]{0:T(1024)} %param.14) | copy-start | bytes 49156
  79.9 2.4 %copy-start = (f32[30,4096]{1,0:T(8,128)S(1)}, f32[30,4096]{1,0:T(8,128)}, u32[]{:S(2)}) copy-start(f32[30,4096]{1,0:T(8,128)} %param.12) | copy-start | bytes 1474564
  79.9 2.4 %copy-start.1 = (f32[4096,30]{0,1:T(8,128)S(1)}, f32[4096,30]{0,1:T(8,128)}, u32[]{:S(2)}) copy-start(f32[4096,30]{0,1:T(8,128)} %copy.77) | copy-start | bytes 1474564
  79.9 2.4 %copy-start.5 = (f32[4096]{0:T(1024)S(1)}, f32[4096]{0:T(1024)}, u32[]{:S(2)}) copy-start(f32[4096]{0:T(1024)} %param.13) | copy-start | bytes 49156
where the time goes:
time: 160 us; the launch traced here: 159 us
  local copies, waits for them, and re-layouts  64 us (40%)
  other arithmetic  51.3 us (32%)
  blocking collectives  21.3 us (13%)
  starting transfers between devices  16.5 us (10%)
  waiting for transfers between devices  4.86 us (3%)
    scatter-add x1, other arithmetic, on_device(): jnp.zeros((species + 1, slot_count), jnp.float32).at[:, particle_slots]  23.2 us
    scatter-add x1, other arithmetic, on_device(): jnp.zeros((species + 1, cell_count), jnp.float32).at[:, flat_list]  22.9 us
    all_to_all x1, blocking collectives, on_device(): lax.all_to_all(moments, ('gx', 'gy'), split_axis=1, concat_axis=1, tiled=...  21.3 us
    gather x2, local copies, waits for them, and re-layouts, on_device(): mates = jnp.take(compositions, partners, axis=1)  17.2 us
    gather x2, local copies, waits for them, and re-layouts, on_device(): local_means = jnp.take(received, particle_slots, axis=1)  16.5 us
    gather x2, local copies, waits for them, and re-layouts, on_device(): outgoing = jnp.take(fields, flat_list, axis=1)  16.4 us
    all_to_all x1, starting transfers between devices, on_device(): lax.all_to_all(outgoing, ('gx', 'gy'), split_axis=1, concat_axis=1, tiled...  7.72 us
    ppermute x2, starting transfers between devices, with_halo(): before = lax.ppermute(last, axis, up)  6.17 us
  transfers between devices with their start and end apart: 5, of which 2 were waited for; matrix products, arithmetic and copies ran while one was open for 14% of the time, Pallas kernels for 0%

commit v1 on v0

v1 whole, which is shorter than its diff:
```python
import functools

import jax
import jax.numpy as jnp
from jax import lax
from jax.experimental import pallas as pl
from jax.experimental.pallas import tpu as pltpu
from jax.sharding import PartitionSpec as P

PAIR_RATE = 0.3
LANES = 128
ROWS = 32
GROUPS = ROWS // 8
F32 = jnp.float32
BF16 = jnp.bfloat16


def pick(table, count, index, start=0, sums=None):
    lane = jnp.broadcast_to(index & (LANES - 1), (8, LANES))
    chunk = jnp.broadcast_to(index >> 7, (8, LANES))
    if sums is None:
        sums = tuple(jnp.zeros((8, LANES), F32) for _ in range(GROUPS))

    def step(at, sums):
        mask = chunk == at
        return tuple(
            jnp.where(
                mask,
                jnp.take_along_axis(
                    table[at, 8 * g : 8 * g + 8, :], lane, axis=1, mode="promise_in_bounds"
                ),
                total,
            )
            for g, total in enumerate(sums)
        )

    return lax.fori_loop(start, start + count, step, sums, unroll=min(count, 16))


def stencil(cells, halo, diffusion, fields, rows_x, rows_y):
    lane = lax.broadcasted_iota(jnp.int32, (ROWS, LANES), 1)
    for x in range(rows_x):
        for y in range(rows_y):
            mid = cells[x, y]
            total = cells[x + 1, y] if x + 1 < rows_x else halo[1, y]
            total = total + (cells[x - 1, y] if x else halo[0, y])
            total = total + (cells[x, y + 1] if y + 1 < rows_y else halo[3, x])
            total = total + (cells[x, y - 1] if y else halo[2, x])
            total = total + jnp.where(lane < LANES - 1, pltpu.roll(mid, LANES - 1, 1), 0.0)
            total = total + jnp.where(lane > 0, pltpu.roll(mid, 1, 1), 0.0)
            j = x * rows_y + y
            fields[j] = mid + diffusion[j : j + 1, :] * (total - 6.0 * mid)


def split_store(values, high, low, at):
    first = values.astype(BF16)
    high[:, pl.ds(at, LANES)] = first
    low[:, pl.ds(at, LANES)] = (values - first.astype(F32)).astype(BF16)


def scatter_block(index, high, low, left, acc, groups, first):
    width = index.shape[1]
    group = (index >> 8).astype(F32).astype(BF16)
    group = jnp.broadcast_to(group, (ROWS, width))
    for g in range(groups):
        mask = group == jnp.array(g, BF16)
        zero = jnp.zeros((ROWS, width), BF16)
        left[2 * g * ROWS : (2 * g + 1) * ROWS, :] = jnp.where(mask, high, zero)
        left[(2 * g + 1) * ROWS : (2 * g + 2) * ROWS, :] = jnp.where(mask, low, zero)
    place = lax.broadcasted_iota(jnp.int32, (256, width), 0)
    right = jnp.where(place == (index & 255), 1.0, 0.0).astype(BF16)
    part = lax.dot_general(
        left[...], right, (((1,), (1,)), ((), ())), preferred_element_type=F32
    )
    if first:
        acc[...] = part
    else:
        acc[...] += part


def acc_row(acc, j):
    g, half = j // 2, (j % 2) * LANES
    return (
        acc[2 * g * ROWS : (2 * g + 1) * ROWS, half : half + LANES]
        + acc[(2 * g + 1) * ROWS : (2 * g + 2) * ROWS, half : half + LANES]
    )


def load_cells(means, cells, rows_x, rows_y):
    species = means.shape[0] // (rows_x * rows_y)
    for x in range(rows_x):
        for y in range(rows_y):
            j = x * rows_y + y
            cells[x, y, 0:species, :] = means[pl.ds(j, species, stride=rows_x * rows_y), :]
            cells[x, y, species:ROWS, :] = jnp.zeros((ROWS - species, LANES), F32)


def send_kernel(rows_x, rows_y, means, halo, diffusion, rate, lists, fields, outgoing, cells):
    species = means.shape[0] // (rows_x * rows_y)
    load_cells(means, cells, rows_x, rows_y)
    stencil(cells, halo, diffusion, fields, rows_x, rows_y)
    count = rows_x * rows_y
    blend = 1.0 - jnp.exp(-rate[...])
    for j in range(count):
        fields[j, species : species + 1, :] = blend[j : j + 1, :]

    def body(d, _):
        parts = pick(fields, count, lists[pl.ds(d, 1), :])
        for g in range(GROUPS):
            outgoing[d, 8 * g : 8 * g + 8, :] = parts[g]
        return 0

    lax.fori_loop(0, lists.shape[0], body, 0)


def mates_kernel(compositions, partners, mates, table):
    species = compositions.shape[0]
    count = compositions.shape[1] // LANES
    for b in range(count):
        table[b, 0:species, :] = compositions[:, b * LANES : (b + 1) * LANES]
        table[b, species:ROWS, :] = jnp.zeros((ROWS - species, LANES), F32)

    def body(b, _):
        parts = pick(table, count, partners[pl.ds(b, 1), :])
        for g in range(GROUPS):
            rows = slice(8 * g, 8 * g + 8)
            mine = table[b, rows, :]
            mates[b, rows, :] = PAIR_RATE * (mine - parts[g])
        return 0

    lax.fori_loop(0, count, body, 0)


def mix_kernel(compositions, received, pair, weights, slots, new, moments, high, low, left, acc):
    species = compositions.shape[0]
    blocks = slots.shape[0]
    chunks = received.shape[0]

    def body(b, _):
        at = pl.multiple_of(b * LANES, LANES)
        parts = pick(received, chunks, slots[pl.ds(b, 1), :])
        local = jnp.concatenate(parts, 0)
        mine = compositions[:, pl.ds(at, LANES)]
        fresh = mine - local[species : species + 1] * (mine - local[:species])
        fresh = fresh - pair[b, 0:species, :]
        new[:, pl.ds(at, LANES)] = fresh
        weight = weights[pl.ds(b, 1), :]
        values = jnp.concatenate(
            [weight * fresh, weight, jnp.zeros((ROWS - species - 1, LANES), F32)], 0
        )
        split_store(values, high, low, at)
        return 0

    lax.fori_loop(0, blocks, body, 0)
    per = left.shape[1] // LANES
    for k in range(blocks // per):
        index = jnp.concatenate([slots[k * per + i : k * per + i + 1, :] for i in range(per)], 1)
        cols = slice(k * per * LANES, (k + 1) * per * LANES)
        scatter_block(index, high[:, cols], low[:, cols], left, acc, chunks // 2, k == 0)
    for s in range(chunks):
        moments[s] = acc_row(acc, s)


def means_kernel(returned, lists, fields, out, high, low, left, acc):
    blocks, count = returned.shape[0], fields.shape[0]
    species = out.shape[0] // count
    for b in range(blocks):
        split_store(returned[b], high, low, b * LANES)
    per = left.shape[1] // LANES
    for k in range(blocks // per):
        index = jnp.concatenate([lists[k * per + i : k * per + i + 1, :] for i in range(per)], 1)
        cols = slice(k * per * LANES, (k + 1) * per * LANES)
        scatter_block(index, high[:, cols], low[:, cols], left, acc, count // 2, k == 0)
    for j in range(count):
        total = acc_row(acc, j)
        mean = (total[:species] + fields[j, 0:species, :]) / (total[species : species + 1] + 1.0)
        out[pl.ds(j, species, stride=count), :] = mean


def call(kernel, name, out_shape, scratch, *args):
    return pl.pallas_call(
        kernel,
        out_shape=out_shape,
        name=name,
        scratch_shapes=scratch,
        compiler_params=pltpu.CompilerParams(vmem_limit_bytes=40 * 1024 * 1024),
    )(*args)


def shift(block, axis, up):
    n = lax.axis_size(axis)
    pairs = [(i, i + 1) if up else (i + 1, i) for i in range(n - 1)]
    return lax.ppermute(block, axis, pairs)


def on_device(
    cell_means, diffusion, mix_rate, send_lists, compositions, weights, particle_slots, partners
):
    species, rows_x, rows_y, depth = cell_means.shape
    count = rows_x * rows_y
    tiles = send_lists.shape[1]
    particles = compositions.shape[1]
    blocks = particles // LANES
    sds = lambda *shape: jax.ShapeDtypeStruct(shape, F32)
    halo = jnp.stack(
        [
            shift(cell_means[:, -1], "gx", True),
            shift(cell_means[:, 0], "gx", False),
            shift(cell_means[:, :, -1], "gy", True),
            shift(cell_means[:, :, 0], "gy", False),
        ]
    ).transpose(0, 2, 1, 3)
    halo = jnp.pad(halo, ((0, 0), (0, 0), (0, ROWS - species), (0, 0)))
    lists = send_lists[0]
    fields, outgoing = call(
        functools.partial(send_kernel, rows_x, rows_y),
        "send_kernel",
        (sds(count, ROWS, LANES), sds(tiles, ROWS, LANES)),
        [pltpu.VMEM((rows_x, rows_y, ROWS, LANES), F32)],
        cell_means.reshape(species * count, depth),
        halo,
        diffusion.reshape(count, depth),
        mix_rate.reshape(count, depth),
        lists,
    )
    received = lax.all_to_all(outgoing, ("gx", "gy"), split_axis=0, concat_axis=0, tiled=True)
    pair = call(
        mates_kernel,
        "mates_kernel",
        sds(blocks, ROWS, LANES),
        [pltpu.VMEM((blocks, ROWS, LANES), F32)],
        compositions,
        partners.reshape(blocks, LANES),
    )
    width = 512
    new, moments = call(
        mix_kernel,
        "mix_kernel",
        (sds(species, particles), sds(tiles, ROWS, LANES)),
        [
            pltpu.VMEM((ROWS, particles), BF16),
            pltpu.VMEM((ROWS, particles), BF16),
            pltpu.VMEM((tiles * ROWS, width), BF16),
            pltpu.VMEM((tiles * ROWS, 256), F32),
        ],
        compositions,
        received,
        pair,
        weights.reshape(blocks, LANES),
        particle_slots.reshape(blocks, LANES),
    )
    returned = lax.all_to_all(moments, ("gx", "gy"), split_axis=0, concat_axis=0, tiled=True)
    out = call(
        means_kernel,
        "means_kernel",
        sds(species * count, LANES),
        [
            pltpu.VMEM((ROWS, tiles * LANES), BF16),
            pltpu.VMEM((ROWS, tiles * LANES), BF16),
            pltpu.VMEM((count * ROWS, width), BF16),
            pltpu.VMEM((count * ROWS, 256), F32),
        ],
        returned,
        lists,
        fields,
    )
    return out.reshape(species, rows_x, rows_y, depth), new


def solution(mesh):
    in_specs = (
        P(None, "gx", "gy", None),
        P("gx", "gy", None),
        P("gx", "gy", None),
        P(("gx", "gy"), None, None),
        P(None, ("gx", "gy")),
        P(("gx", "gy")),
        P(("gx", "gy")),
        P(("gx", "gy")),
    )
    out_specs = (P(None, "gx", "gy", None), P(None, ("gx", "gy")))
    return jax.shard_map(
        on_device, mesh=mesh, in_specs=in_specs, out_specs=out_specs, check_vma=False
    )
```

time: 160 us -> 77.6 us (0.48)
  local copies, waits for them, and re-layouts: 64 us -> 1.99 us
  other arithmetic: 51.3 us -> 0.02 us
  Pallas kernels: 0 us -> 28.4 us
  waiting for transfers between devices: 4.86 us -> 9.27 us
  blocking collectives: 21.3 us -> 18.4 us
  starting transfers between devices: 16.5 us -> 18.2 us
    gather x6 -> x0, local copies, waits for them, and re-layouts: 50 us -> none  [the longest x2 17.2 us: on_device(): mates = jnp.take(compositions, partners, axis=1)]
    scatter-add x2 -> x0, other arithmetic: 46.1 us -> none  [the longest x1 23.2 us: on_device(): jnp.zeros((species + 1, slot_count), jnp.float32).at[:, particle_slots]]
    pallas_call x0 -> x4, Pallas kernels: none -> 28.4 us  [call(): pl.pallas_call(kernel, out_shape=out_shape, name=name, scratch_shapes=scr...]
    all_to_all x1, waiting for transfers between devices: 0.01 us -> 6.49 us  [on_device(): lax.all_to_all(outgoing, ('gx', 'gy'), split_axis=0, concat_axis=0, tiled...]
    all_to_all x4 -> x0, local copies, waits for them, and re-layouts: 5.4 us -> none  [the longest x3 3.74 us: on_device(): lax.all_to_all(moments, ('gx', 'gy'), split_axis=1, concat_axis=1, tiled=...]
    unnamed x20, local copies, waits for them, and re-layouts: 4.07 us -> 0.73 us
    all_to_all x1, blocking collectives: 21.3 us -> 18.4 us  [on_device(): lax.all_to_all(moments, ('gx', 'gy'), split_axis=0, concat_axis=0, tiled=...]
    ppermute x4, starting transfers between devices: 8.75 us -> 11.1 us  [shift(): return lax.ppermute(block, axis, pairs)]
  transfers between devices with their start and end apart: 5 -> 5, of which waited for: 2 -> 3; matrix products, arithmetic and copies ran while one was open for 14% -> 0% of each run, Pallas kernels for 0% -> 12%
where the time goes in v1:
time: 77.6 us; the launch traced here: 77.1 us
  Pallas kernels  28.4 us (37%)
  blocking collectives  18.4 us (24%)
  starting transfers between devices  18.2 us (23%)
  waiting for transfers between devices  9.27 us (12%)
  local copies, waits for them, and re-layouts  1.99 us (3%)
  between operations  0.83 us (1%)
    pallas_call x4, Pallas kernels, call(): pl.pallas_call(kernel, out_shape=out_shape, name=name, scratch_shapes=scr...  28.4 us
    all_to_all x1, blocking collectives, on_device(): lax.all_to_all(moments, ('gx', 'gy'), split_axis=0, concat_axis=0, tiled=...  18.4 us
    ppermute x4, starting transfers between devices, shift(): return lax.ppermute(block, axis, pairs)  11.1 us
    all_to_all x1, starting transfers between devices, on_device(): lax.all_to_all(outgoing, ('gx', 'gy'), split_axis=0, concat_axis=0, tiled...  7.12 us
    all_to_all x1, waiting for transfers between devices, on_device(): lax.all_to_all(outgoing, ('gx', 'gy'), split_axis=0, concat_axis=0, tiled...  6.49 us
    ppermute x4, waiting for transfers between devices, shift(): return lax.ppermute(block, axis, pairs)  2.78 us
  transfers between devices with their start and end apart: 5, of which 3 were waited for; matrix products, arithmetic and copies ran while one was open for 0% of the time, Pallas kernels for 12%

profile of v1, /device:TPU:0, one launch (start us, length us, event | category | flops | bytes accessed | tf_op | source)
XLA Modules:
  0.0 77.1 jit_solution(15197218966412654364)
XLA Ops:
  0.6 0.0 copy-start.1
  0.6 1.2 %fusion.1 = (f32[30,4,1,128]{3,2,1,0:T(1,128)S(1)}, f32[30,4,1,128]{3,2,1,0:T(1,128)S(1)}) fusion(f32[30,4,4,128]{3,2,1,0:T(4,128)} %param.8), kind=kLoop, calls=%fused_computation.6 | loop fusion | bytes 245760 | tf_op jit(solution)/shard_map/slice | solution.py:209
  1.9 1.3 %collective-permute-start.3 = (f32[30,4,128]{2,0,1:T(8,128)S(1)}, f32[30,4,128]{2,0,1:T(8,128)S(1)}, u32[]{:S(2)}, u32[]{:S(2)}) collective-permute-start(f32[30,4,128]{2,0,1:T(8,128)S(1)} %bitcast.35), channel_id=1, source_target_pairs={{1,0},{2,1},{3,2},{5,4},{6,5},{7,6},{9,8},{10,9},{11,10},{13,12},{... | collective-permute-start | bytes 184328 | tf_op jit(solution)/shard_map/ppermute | solution.py:193
  3.2 3.0 %collective-permute-start.2 = (f32[30,4,128]{2,0,1:T(8,128)S(1)}, f32[30,4,128]{2,0,1:T(8,128)S(1)}, u32[]{:S(2)}, u32[]{:S(2)}) collective-permute-start(f32[30,4,128]{2,0,1:T(8,128)S(1)} %bitcast.36), channel_id=1, source_target_pairs={{0,1},{1,2},{2,3},{4,5},{5,6},{6,7},{8,9},{9,10},{10,11},{12,13},{... | collective-permute-start | bytes 184328 | tf_op jit(solution)/shard_map/ppermute | solution.py:193
  6.2 0.0 copy-done.1
  6.3 1.3 %collective-permute-start.1 = (f32[30,4,128]{2,0,1:T(8,128)S(1)}, f32[30,4,128]{2,0,1:T(8,128)S(1)}, u32[]{:S(2)}, u32[]{:S(2)}) collective-permute-start(f32[30,4,128]{2,0,1:T(8,128)S(1)} %bitcast.37), channel_id=1, source_target_pairs={{4,0},{8,4},{12,8},{16,12},{20,16},{24,20},{28,24},{5,1},{9,5},{13... | collective-permute-start | bytes 184328 | tf_op jit(solution)/shard_map/ppermute | solution.py:193
  7.6 5.5 %collective-permute-start = (f32[30,4,128]{2,0,1:T(8,128)S(1)}, f32[30,4,128]{2,0,1:T(8,128)S(1)}, u32[]{:S(2)}, u32[]{:S(2)}) collective-permute-start(f32[30,4,128]{2,0,1:T(8,128)S(1)} %bitcast.38), channel_id=1, source_target_pairs={{0,4},{4,8},{8,12},{12,16},{16,20},{20,24},{24,28},{1,5},{5,9},{9,... | collective-permute-start | bytes 184328 | tf_op jit(solution)/shard_map/ppermute | solution.py:193
  13.1 0.0 collective-permute-done.3
  13.1 0.0 collective-permute-done.2
  13.1 0.4 collective-permute-done.1
  13.5 2.4 %collective-permute-done = f32[30,4,128]{2,0,1:T(8,128)S(1)} collective-permute-done((f32[30,4,128]{2,0,1:T(8,128)S(1)}, f32[30,4,128]{2,0,1:T(8,128)S(1)}, u32[]{:S(2)}, u32[]{:S(2)}) %collective-permute-start) | collective-permute-done | bytes 61472 | tf_op jit(solution)/shard_map/ppermute | solution.py:193
  15.9 0.0 copy-start.2
  15.9 0.0 copy-start.6
  15.9 0.0 copy-start.7
  16.0 0.7 copy-done.2
  16.6 0.0 copy-done.6
  16.6 0.0 copy-done.7
  16.7 5.5 %send_kernel.1 = (f32[16,32,128]{2,1,0:T(8,128)S(1)}, f32[32,32,128]{2,1,0:T(8,128)}) custom-call(f32[480,128]{1,0:T(8,128)S(1)} %bitcast.26, f32[4,4,32,128]{3,2,1,0:T(8,128)S(1)} %pad.4.halo, f32[16,128]{1,0:T(8,128)S(1)} %bitcast.32, f32[16,128]{1,0:T(8,128)S(1)} %bitcast.33, s32[32,128]{1,0:T(8,128)S(1)} %bitcast.27), custom_call_target="tpu_custom_call" | custom-call | tf_op jit(solution)/shard_map/send_kernel/pallas_call | solution.py:181
  22.2 0.0 copy-start
  22.2 0.0 copy-start.3
  22.2 7.1 %all-to-all-start = ((f32[32,32,128]{2,1,0:T(8,128)}), f32[32,32,128]{2,1,0:T(8,128)S(1)}, u32[]{:S(2)}, u32[]{:S(2)}) async-start(f32[32,32,128]{2,1,0:T(8,128)} %get-tuple-element.6), calls=%async_computation | async-start | bytes 1048576 | tf_op jit(solution)/shard_map/all_to_all | solution.py:226
  29.3 0.0 copy-done
  29.3 0.0 copy-done.3
  29.3 0.0 copy-start.4
  29.3 0.0 copy-start.5
  29.4 9.0 %mates_kernel.1.pair = f32[32,32,128]{2,1,0:T(8,128)S(1)} custom-call(f32[30,4096]{1,0:T(8,128)S(1)} %copy-done, s32[32,128]{1,0:T(8,128)S(1)} %bitcast.29), custom_call_target="tpu_custom_call" | custom-call | tf_op jit(solution)/shard_map/mates_kernel/pallas_call | solution.py:181
  38.4 6.5 %all-to-all-done.received = f32[32,32,128]{2,1,0:T(8,128)S(1)} async-done(((f32[32,32,128]{2,1,0:T(8,128)}), f32[32,32,128]{2,1,0:T(8,128)S(1)}, u32[]{:S(2)}, u32[]{:S(2)}) %all-to-all-start) | async-done | bytes 524320 | tf_op jit(solution)/shard_map/all_to_all | solution.py:226
  44.9 0.0 copy-done.4
  44.9 0.0 copy-done.5
  44.9 11.7 %mix_kernel.1 = (f32[30,4096]{1,0:T(8,128)}, f32[32,32,128]{2,1,0:T(8,128)S(1)}) custom-call(f32[30,4096]{1,0:T(8,128)S(1)} %copy-done, f32[32,32,128]{2,1,0:T(8,128)S(1)} %all-to-all-done.received, f32[32,32,128]{2,1,0:T(8,128)S(1)} %mates_kernel.1.pair, f32[32,128]{1,0:T(8,128)S(1)} %bitcast.30, s32[32,128]{1,0:T(8,128)S(1)} %bitcast.31), custom_call_target="tpu_custom_call" | custom-call | tf_op jit(solution)/shard_map/mix_kernel/pallas_call | solution.py:181
  56.6 18.4 %all_to_all.10.returned = f32[32,32,128]{2,1,0:T(8,128)S(1)} all-to-all(f32[32,32,128]{2,1,0:T(8,128)S(1)} %get-tuple-element.7), channel_id=1, replica_groups=mesh['gx'=8,'gy'=4] {'gx','gy'}, dimensions={0} | all-to-all | bytes 1048576 | tf_op jit(solution)/shard_map/all_to_all | solution.py:252
  75.0 2.1 %means_kernel.1 = f32[480,128]{1,0:T(8,128)} custom-call(f32[32,32,128]{2,1,0:T(8,128)S(1)} %all_to_all.10.returned, s32[32,128]{1,0:T(8,128)S(1)} %bitcast.28, f32[16,32,128]{2,1,0:T(8,128)S(1)} %get-tuple-element.8.fields), custom_call_target="tpu_custom_call" | custom-call | tf_op jit(solution)/shard_map/means_kernel/pallas_call | solution.py:181
  (7 shorter events, 0.1 us)
Async XLA Ops:
  0.6 5.6 %copy-start.1 = (f32[30,4,4,128]{3,2,1,0:T(4,128)S(1)}, f32[30,4,4,128]{3,2,1,0:T(4,128)}, u32[]{:S(2)}) copy-start(f32[30,4,4,128]{3,2,1,0:T(4,128)} %param.8) | copy-start | bytes 737284
  1.9 11.2 %collective-permute-start.3 = (f32[30,4,128]{2,0,1:T(8,128)S(1)}, f32[30,4,128]{2,0,1:T(8,128)S(1)}, u32[]{:S(2)}, u32[]{:S(2)}) collective-permute-start(f32[30,4,128]{2,0,1:T(8,128)S(1)} %bitcast.35), channel_id=1, source_target_pairs={{1,0},{2,1},{3,2},{5,4},{6,5},{7,6},{9,8},{10,9},{11,10},{13,12},{... | collective-permute-start | bytes 184328 | tf_op jit(solution)/shard_map/ppermute | solution.py:193
  3.2 9.9 %collective-permute-start.2 = (f32[30,4,128]{2,0,1:T(8,128)S(1)}, f32[30,4,128]{2,0,1:T(8,128)S(1)}, u32[]{:S(2)}, u32[]{:S(2)}) collective-permute-start(f32[30,4,128]{2,0,1:T(8,128)S(1)} %bitcast.36), channel_id=1, source_target_pairs={{0,1},{1,2},{2,3},{4,5},{5,6},{6,7},{8,9},{9,10},{10,11},{12,13},{... | collective-permute-start | bytes 184328 | tf_op jit(solution)/shard_map/ppermute | solution.py:193
  6.3 7.2 %collective-permute-start.1 = (f32[30,4,128]{2,0,1:T(8,128)S(1)}, f32[30,4,128]{2,0,1:T(8,128)S(1)}, u32[]{:S(2)}, u32[]{:S(2)}) collective-permute-start(f32[30,4,128]{2,0,1:T(8,128)S(1)} %bitcast.37), channel_id=1, source_target_pairs={{4,0},{8,4},{12,8},{16,12},{20,16},{24,20},{28,24},{5,1},{9,5},{13... | collective-permute-start | bytes 184328 | tf_op jit(solution)/shard_map/ppermute | solution.py:193
  7.6 8.3 %collective-permute-start = (f32[30,4,128]{2,0,1:T(8,128)S(1)}, f32[30,4,128]{2,0,1:T(8,128)S(1)}, u32[]{:S(2)}, u32[]{:S(2)}) collective-permute-start(f32[30,4,128]{2,0,1:T(8,128)S(1)} %bitcast.38), channel_id=1, source_target_pairs={{0,4},{4,8},{8,12},{12,16},{16,20},{20,24},{24,28},{1,5},{5,9},{9,... | collective-permute-start | bytes 184328 | tf_op jit(solution)/shard_map/ppermute | solution.py:193
  15.9 0.7 copy-start.2
  15.9 0.7 copy-start.6
  15.9 0.7 copy-start.7
  22.2 7.1 %copy-start = (f32[30,4096]{1,0:T(8,128)S(1)}, f32[30,4096]{1,0:T(8,128)}, u32[]{:S(2)}) copy-start(f32[30,4096]{1,0:T(8,128)} %compositions.3) | copy-start | bytes 1474564
  22.2 7.1 %copy-start.3 = (s32[4096]{0:T(1024)S(1)}, s32[4096]{0:T(1024)}, u32[]{:S(2)}) copy-start(s32[4096]{0:T(1024)} %param.15) | copy-start | bytes 49156
  22.2 22.7 %all-to-all-start = ((f32[32,32,128]{2,1,0:T(8,128)}), f32[32,32,128]{2,1,0:T(8,128)S(1)}, u32[]{:S(2)}, u32[]{:S(2)}) async-start(f32[32,32,128]{2,1,0:T(8,128)} %get-tuple-element.6), calls=%async_computation | async-start | bytes 1048576 | tf_op jit(solution)/shard_map/all_to_all | solution.py:226
  29.3 15.5 %copy-start.4 = (f32[4096]{0:T(1024)S(1)}, f32[4096]{0:T(1024)}, u32[]{:S(2)}) copy-start(f32[4096]{0:T(1024)} %param.13) | copy-start | bytes 49156
  29.3 15.5 %copy-start.5 = (s32[4096]{0:T(1024)S(1)}, s32[4096]{0:T(1024)}, u32[]{:S(2)}) copy-start(s32[4096]{0:T(1024)} %param.14) | copy-start | bytes 49156

commit v2 on v1

v2 whole, which is shorter than its diff:
```python
import functools

import jax
import jax.numpy as jnp
from jax import lax
from jax.experimental import pallas as pl
from jax.experimental.pallas import tpu as pltpu
from jax.sharding import PartitionSpec as P

PAIR_RATE = 0.3
LANES = 128
ROWS = 32
GROUPS = ROWS // 8
F32 = jnp.float32
BF16 = jnp.bfloat16


def pick(table, count, index, start=0, sums=None):
    lane = jnp.broadcast_to(index & (LANES - 1), (8, LANES))
    chunk = jnp.broadcast_to(index >> 7, (8, LANES))
    if sums is None:
        sums = tuple(jnp.zeros((8, LANES), F32) for _ in range(GROUPS))

    def step(at, sums):
        mask = chunk == at
        return tuple(
            jnp.where(
                mask,
                jnp.take_along_axis(
                    table[at, 8 * g : 8 * g + 8, :], lane, axis=1, mode="promise_in_bounds"
                ),
                total,
            )
            for g, total in enumerate(sums)
        )

    return lax.fori_loop(start, start + count, step, sums, unroll=min(count, 16))


def stencil(cells, halo, diffusion, fields, rows_x, rows_y):
    lane = lax.broadcasted_iota(jnp.int32, (ROWS, LANES), 1)
    for x in range(rows_x):
        for y in range(rows_y):
            mid = cells[x, y]
            total = cells[x + 1, y] if x + 1 < rows_x else halo[1, y]
            total = total + (cells[x - 1, y] if x else halo[0, y])
            total = total + (cells[x, y + 1] if y + 1 < rows_y else halo[3, x])
            total = total + (cells[x, y - 1] if y else halo[2, x])
            total = total + jnp.where(lane < LANES - 1, pltpu.roll(mid, LANES - 1, 1), 0.0)
            total = total + jnp.where(lane > 0, pltpu.roll(mid, 1, 1), 0.0)
            j = x * rows_y + y
            fields[j] = mid + diffusion[j : j + 1, :] * (total - 6.0 * mid)


def scatter_block(index, high, low, left, acc, groups):
    width = index.shape[1]
    group = (index >> 8).astype(F32).astype(BF16)
    group = jnp.broadcast_to(group, (ROWS, width))
    for g in range(groups):
        mask = group == jnp.array(g, BF16)
        zero = jnp.zeros((ROWS, width), BF16)
        left[2 * g * ROWS : (2 * g + 1) * ROWS, :] = jnp.where(mask, high, zero)
        left[(2 * g + 1) * ROWS : (2 * g + 2) * ROWS, :] = jnp.where(mask, low, zero)
    place = lax.broadcasted_iota(jnp.int32, (256, width), 0)
    right = jnp.where(place == (index & 255), 1.0, 0.0).astype(BF16)
    part = lax.dot_general(
        left[...], right, (((1,), (1,)), ((), ())), preferred_element_type=F32
    )
    acc[...] += part


def acc_row(acc, j):
    g, half = j // 2, (j % 2) * LANES
    return (
        acc[2 * g * ROWS : (2 * g + 1) * ROWS, half : half + LANES]
        + acc[(2 * g + 1) * ROWS : (2 * g + 2) * ROWS, half : half + LANES]
    )


def load_cells(means, cells, rows_x, rows_y):
    species = means.shape[0] // (rows_x * rows_y)
    for x in range(rows_x):
        for y in range(rows_y):
            j = x * rows_y + y
            cells[x, y, 0:species, :] = means[pl.ds(j, species, stride=rows_x * rows_y), :]
            cells[x, y, species:ROWS, :] = jnp.zeros((ROWS - species, LANES), F32)


def gather_pairs(compositions, partners, table, parts, pair):
    species, particles = compositions.shape
    groups = particles // 256
    for h in range(groups):
        values = compositions[:, h * 256 : (h + 1) * 256]
        values = jnp.concatenate([values, jnp.zeros((ROWS - species, 256), F32)], 0)
        first = values.astype(BF16)
        table[h * ROWS : (h + 1) * ROWS, 0:256] = first
        table[h * ROWS : (h + 1) * ROWS, 256:512] = (values - first.astype(F32)).astype(BF16)

    def body(k, _):
        index = jnp.concatenate([partners[pl.ds(2 * k + i, 1), :] for i in range(2)], 1)
        place = lax.broadcasted_iota(jnp.int32, (256, 256), 0)
        hot = jnp.where(place == (index & 255), 1.0, 0.0).astype(BF16)
        hot = jnp.concatenate([hot, hot], 0)
        parts[...] = jnp.dot(table[...], hot, preferred_element_type=F32)
        group = jnp.broadcast_to(index >> 8, (ROWS, 256))
        total = jnp.zeros((ROWS, 256), F32)
        for h in range(groups):
            total = jnp.where(group == h, parts[h * ROWS : (h + 1) * ROWS, :], total)
        at = pl.multiple_of(k * 256, 256)
        pair[0:species, pl.ds(at, 256)] = PAIR_RATE * (
            compositions[:, pl.ds(at, 256)] - total[:species]
        )
        return 0

    lax.fori_loop(0, particles // 256, body, 0)


def whole_kernel(
    nx, ny, rows_x, rows_y,
    means, diffusion, rate, lists, compositions, weights, slots, partners,
    out, new,
    cells, halo, fields, outgoing, received, local, moments, returned,
    table, parts, pair, high, low, left1, acc1, left2, acc2,
    halo_send, halo_recv, go_send, go_recv, back_send, back_recv,
):
    tiles = nx * ny
    half = tiles // 2
    count = rows_x * rows_y
    species = compositions.shape[0]
    blocks = slots.shape[0]
    gx, gy = lax.axis_index("gx"), lax.axis_index("gy")
    me = gx * ny + gy

    def place(d):
        return (lax.div(d, ny), lax.rem(d, ny))

    barrier = pltpu.get_barrier_semaphore()

    def greet(k, _):
        d = lax.rem(me + k, tiles)
        pl.semaphore_signal(
            barrier, inc=1, device_id=place(d), device_id_type=pl.DeviceIdType.MESH
        )
        return 0

    lax.fori_loop(1, tiles, greet, 0)

    for x in range(rows_x):
        for y in range(rows_y):
            j = x * rows_y + y
            cells[x, y, 0:species, :] = means[pl.ds(j, species, stride=count), :]
            cells[x, y, species:ROWS, :] = jnp.zeros((ROWS - species, LANES), F32)

    pl.semaphore_wait(barrier, tiles - 1)

    def halo_copy(i):
        source, length, target = (
            (cells.at[rows_x - 1], rows_y, (gx + 1, gy)),
            (cells.at[0], rows_y, (gx - 1, gy)),
            (cells.at[:, rows_y - 1], rows_x, (gx, gy + 1)),
            (cells.at[:, 0], rows_x, (gx, gy - 1)),
        )[i]
        return pltpu.make_async_remote_copy(
            src_ref=source,
            dst_ref=halo.at[i, 0:length],
            send_sem=halo_send.at[i],
            recv_sem=halo_recv.at[i],
            device_id=target,
            device_id_type=pl.DeviceIdType.MESH,
        )

    sends = (gx < nx - 1, gx > 0, gy < ny - 1, gy > 0)
    receives = (gx > 0, gx < nx - 1, gy > 0, gy < ny - 1)
    for i in range(4):

        @pl.when(sends[i])
        def _(i=i):
            halo_copy(i).start()

        @pl.when(jnp.logical_not(receives[i]))
        def _(i=i):
            halo[i] = jnp.zeros(halo.shape[1:], F32)

    gather_pairs(compositions, partners, table, parts, pair)

    for i in range(4):

        @pl.when(receives[i])
        def _(i=i):
            halo_copy(i).wait_recv()

    stencil(cells, halo, diffusion, fields, rows_x, rows_y)
    blend = 1.0 - jnp.exp(-rate[...])
    for j in range(count):
        fields[j, species : species + 1, :] = blend[j : j + 1, :]

    def copy_of(buffers, sems, source, d, target):
        return pltpu.make_async_remote_copy(
            src_ref=buffers[0].at[d],
            dst_ref=buffers[1].at[source],
            send_sem=sems[0].at[d],
            recv_sem=sems[1].at[source],
            device_id=place(target),
            device_id_type=pl.DeviceIdType.MESH,
        )

    go = (outgoing, received), (go_send, go_recv)
    back = (moments, returned), (back_send, back_recv)

    def fill(d, buffer, row):
        found = pick(fields, count, lists[pl.ds(d, 1), :])
        for g in range(GROUPS):
            buffer[row, 8 * g : 8 * g + 8, :] = found[g]

    def send_one(k):
        d = lax.rem(me + k, tiles)
        fill(d, outgoing, d)
        copy_of(*go, me, d, d).start()

    lax.fori_loop(0, half, lambda i, _: (send_one(half + i), 0)[1], 0)
    lax.fori_loop(1, half, lambda i, _: (send_one(half - i), 0)[1], 0)
    fill(me, received, me)

    def source_of(k):
        return lax.rem(me + tiles - k, tiles)

    def wait_for(which, k):
        @pl.when(k > 0)
        def _():
            s = source_of(k)
            copy_of(*which, s, s, s).wait_recv()

    step_of = 8

    def arrivals(first_k, sign):
        def batch(n, _):
            ks = [first_k + sign * (n * step_of + i) for i in range(step_of)]
            for k in ks:
                wait_for(go, k)

            def body(b, _):
                index = slots[pl.ds(b, 1), :]
                lane = jnp.broadcast_to(index & (LANES - 1), (8, LANES))
                chunk = jnp.broadcast_to(index >> 7, (8, LANES))
                sums = [local[b, 8 * g : 8 * g + 8, :] for g in range(GROUPS)]
                for k in ks:
                    s = source_of(k)
                    mask = chunk == s
                    for g in range(GROUPS):
                        rows = received[s, 8 * g : 8 * g + 8, :]
                        found = jnp.take_along_axis(
                            rows, lane, axis=1, mode="promise_in_bounds"
                        )
                        sums[g] = jnp.where(mask, found, sums[g])
                for g in range(GROUPS):
                    local[b, 8 * g : 8 * g + 8, :] = sums[g]
                return 0

            lax.fori_loop(0, blocks, body, 0, unroll=2)
            return 0

        lax.fori_loop(0, half // step_of, batch, 0)

    local[...] = jnp.zeros(local.shape, F32)
    arrivals(half, 1)
    arrivals(half - 1, -1)

    def mix(b, _):
        at = pl.multiple_of(b * LANES, LANES)
        mine = compositions[:, pl.ds(at, LANES)]
        fresh = mine - local[b, species : species + 1, :] * (mine - local[b, 0:species, :])
        fresh = fresh - pair[0:species, pl.ds(at, LANES)]
        new[:, pl.ds(at, LANES)] = fresh
        weight = weights[pl.ds(b, 1), :]
        values = jnp.concatenate(
            [weight * fresh, weight, jnp.zeros((ROWS - species - 1, LANES), F32)], 0
        )
        first = values.astype(BF16)
        high[:, pl.ds(at, LANES)] = first
        low[:, pl.ds(at, LANES)] = (values - first.astype(F32)).astype(BF16)
        return 0

    lax.fori_loop(0, blocks, mix, 0, unroll=2)
    acc1[...] = jnp.zeros(acc1.shape, F32)
    per = left1.shape[1] // LANES

    def gather_moments(k, _):
        index = jnp.concatenate([slots[pl.ds(k * per + i, 1), :] for i in range(per)], 1)
        at = pl.multiple_of(k * per * LANES, per * LANES)
        cols = pl.ds(at, per * LANES)
        scatter_block(index, high[:, cols], low[:, cols], left1, acc1, half)
        return 0

    lax.fori_loop(0, blocks // per, gather_moments, 0)
    for s in range(tiles):
        moments[s] = acc_row(acc1, s)

    def return_one(k):
        d = lax.rem(me + k, tiles)
        copy_of(*back, me, d, d).start()

    lax.fori_loop(0, half, lambda i, _: (return_one(half + i), 0)[1], 0)
    lax.fori_loop(1, half, lambda i, _: (return_one(half - i), 0)[1], 0)
    returned[me] = moments[me]

    acc2[...] = jnp.zeros(acc2.shape, F32)
    per2 = left2.shape[1] // LANES

    def returns(first_k, sign):
        def batch(n, _):
            ks = [first_k + sign * (n * per2 + i) for i in range(per2)]
            for k in ks:
                wait_for(back, k)
            values = jnp.concatenate([returned[source_of(k)] for k in ks], 1)
            index = jnp.concatenate([lists[pl.ds(source_of(k), 1), :] for k in ks], 1)
            first = values.astype(BF16)
            second = (values - first.astype(F32)).astype(BF16)
            scatter_block(index, first, second, left2, acc2, count // 2)
            return 0

        lax.fori_loop(0, half // per2, batch, 0)

    returns(half, 1)
    returns(half - 1, -1)
    for j in range(count):
        total = acc_row(acc2, j)
        mean = (total[:species] + fields[j, 0:species, :]) / (total[species : species + 1] + 1.0)
        out[pl.ds(j, species, stride=count), :] = mean

    for i in range(4):

        @pl.when(sends[i])
        def _(i=i):
            halo_copy(i).wait_send()

    def finish(k, _):
        d = lax.rem(me + k, tiles)
        copy_of(*go, me, d, d).wait_send()
        copy_of(*back, me, d, d).wait_send()
        return 0

    lax.fori_loop(1, tiles, finish, 0)


def on_device(
    cell_means, diffusion, mix_rate, send_lists, compositions, weights, particle_slots, partners
):
    species, rows_x, rows_y, depth = cell_means.shape
    count = rows_x * rows_y
    tiles = send_lists.shape[1]
    particles = compositions.shape[1]
    blocks = particles // LANES
    width = 512
    vmem = lambda *shape: pltpu.VMEM(shape, F32)
    half_vmem = lambda *shape: pltpu.VMEM(shape, BF16)
    out, new = pl.pallas_call(
        functools.partial(
            whole_kernel, lax.axis_size("gx"), lax.axis_size("gy"), rows_x, rows_y
        ),
        out_shape=(
            jax.ShapeDtypeStruct((species * count, LANES), F32),
            jax.ShapeDtypeStruct((species, particles), F32),
        ),
        in_specs=[pl.BlockSpec(memory_space=pltpu.VMEM)] * 8,
        out_specs=[pl.BlockSpec(memory_space=pltpu.VMEM)] * 2,
        name="whole_kernel",
        scratch_shapes=[
            vmem(rows_x, rows_y, ROWS, LANES),
            vmem(4, max(rows_x, rows_y), ROWS, LANES),
            vmem(count, ROWS, LANES),
            vmem(tiles, ROWS, LANES),
            vmem(tiles, ROWS, LANES),
            vmem(blocks, ROWS, LANES),
            vmem(tiles, ROWS, LANES),
            vmem(tiles, ROWS, LANES),
            half_vmem(particles // 256 * ROWS, 512),
            vmem(particles // 256 * ROWS, 256),
            vmem(ROWS, particles),
            half_vmem(ROWS, particles),
            half_vmem(ROWS, particles),
            half_vmem(tiles * ROWS, width),
            vmem(tiles * ROWS, 256),
            half_vmem(count * ROWS, width),
            vmem(count * ROWS, 256),
            pltpu.SemaphoreType.DMA((4,)),
            pltpu.SemaphoreType.DMA((4,)),
            pltpu.SemaphoreType.DMA((tiles,)),
            pltpu.SemaphoreType.DMA((tiles,)),
            pltpu.SemaphoreType.DMA((tiles,)),
            pltpu.SemaphoreType.DMA((tiles,)),
        ],
        compiler_params=pltpu.CompilerParams(
            collective_id=0, has_side_effects=True, vmem_limit_bytes=44 * 1024 * 1024
        ),
    )(
        cell_means.reshape(species * count, depth),
        diffusion.reshape(count, depth),
        mix_rate.reshape(count, depth),
        send_lists[0],
        compositions,
        weights.reshape(blocks, LANES),
        particle_slots.reshape(blocks, LANES),
        partners.reshape(blocks, LANES),
    )
    return out.reshape(species, rows_x, rows_y, depth), new


def solution(mesh):
    in_specs = (
        P(None, "gx", "gy", None),
        P("gx", "gy", None),
        P("gx", "gy", None),
        P(("gx", "gy"), None, None),
        P(None, ("gx", "gy")),
        P(("gx", "gy")),
        P(("gx", "gy")),
        P(("gx", "gy")),
    )
    out_specs = (P(None, "gx", "gy", None), P(None, ("gx", "gy")))
    return jax.shard_map(
        on_device, mesh=mesh, in_specs=in_specs, out_specs=out_specs, check_vma=False
    )
```

time: 77.6 us -> 60.4 us (0.78)
  Pallas kernels: 28.4 us -> 51.4 us
  blocking collectives: 18.4 us -> 0 us
  starting transfers between devices: 18.2 us -> 0 us
  waiting for transfers between devices: 9.27 us -> 0 us
  local copies, waits for them, and re-layouts: 1.99 us -> 7.73 us
    pallas_call x4 -> x1, Pallas kernels: 28.4 us -> 51.4 us  [on_device(): pl.pallas_call(functools.partial(whole_kernel, lax.axis_size('gx'), lax.a...]
    all_to_all x1 -> x0, blocking collectives: 18.4 us -> none  [on_device(): lax.all_to_all(moments, ('gx', 'gy'), split_axis=0, concat_axis=0, tiled=...]
    ppermute x4 -> x0, starting transfers between devices: 11.1 us -> none  [shift(): return lax.ppermute(block, axis, pairs)]
    all_to_all x1 -> x0, starting transfers between devices: 7.12 us -> none  [on_device(): lax.all_to_all(outgoing, ('gx', 'gy'), split_axis=0, concat_axis=0, tiled...]
    unnamed x20 -> x18, local copies, waits for them, and re-layouts: 0.73 us -> 7.73 us
    all_to_all x1 -> x0, waiting for transfers between devices: 6.49 us -> none  [on_device(): lax.all_to_all(outgoing, ('gx', 'gy'), split_axis=0, concat_axis=0, tiled...]
    ppermute x4 -> x0, waiting for transfers between devices: 2.78 us -> none  [shift(): return lax.ppermute(block, axis, pairs)]
    slice x2 -> x0, local copies, waits for them, and re-layouts: 1.24 us -> none  [the longest x1 1.21 us: on_device(): cell_means[:, :, -1]]
  transfers between devices with their start and end apart: 5 -> 0, of which waited for: 3 -> 0; matrix products, arithmetic and copies ran while one was open for 0% -> 0% of each run, Pallas kernels for 12% -> 0%
where the time goes in v2:
time: 60.4 us; the launch traced here: 59.8 us
  Pallas kernels  51.4 us (85%)
  local copies, waits for them, and re-layouts  7.73 us (13%)
  between operations  0.66 us (1%)
    pallas_call x1, Pallas kernels, on_device(): pl.pallas_call(functools.partial(whole_kernel, lax.axis_size('gx'), lax.a...  51.4 us
    unnamed x18, local copies, waits for them, and re-layouts  7.73 us

profile of v2, /device:TPU:0, one launch (start us, length us, event | category | flops | bytes accessed | tf_op | source)
XLA Modules:
  0.0 59.8 jit_solution(6327581857354260548)
XLA Ops:
  0.6 0.0 copy-start.6
  0.6 0.7 %copy-done.6 = f32[4,4,128]{2,1,0:T(4,128)S(1)} copy-done((f32[4,4,128]{2,1,0:T(4,128)S(1)}, f32[4,4,128]{2,1,0:T(4,128)}, u32[]{:S(2)}) %copy-start.6) | copy-done | bytes 8216
  1.3 0.0 copy-start
  1.3 1.0 %copy-done = f32[30,4096]{1,0:T(8,128)S(1)} copy-done((f32[30,4096]{1,0:T(8,128)S(1)}, f32[30,4096]{1,0:T(8,128)}, u32[]{:S(2)}) %copy-start) | copy-done | bytes 491544
  2.4 0.0 copy-start.1
  2.4 0.9 %copy-done.1 = f32[30,4,4,128]{3,2,1,0:T(4,128)S(1)} copy-done((f32[30,4,4,128]{3,2,1,0:T(4,128)S(1)}, f32[30,4,4,128]{3,2,1,0:T(4,128)}, u32[]{:S(2)}) %copy-start.1) | copy-done | bytes 245784
  3.3 0.0 copy-start.2
  3.3 0.7 %copy-done.2 = s32[1,32,128]{2,1,0:T(8,128)S(1)} copy-done((s32[1,32,128]{2,1,0:T(8,128)S(1)}, s32[1,32,128]{2,1,0:T(8,128)}, u32[]{:S(2)}) %copy-start.2) | copy-done | bytes 16408
  4.0 0.0 copy-start.3
  4.0 0.7 %copy-done.3 = f32[4096]{0:T(1024)S(1)} copy-done((f32[4096]{0:T(1024)S(1)}, f32[4096]{0:T(1024)}, u32[]{:S(2)}) %copy-start.3) | copy-done | bytes 16408
  4.8 0.0 copy-start.4
  4.8 0.7 %copy-done.4 = s32[4096]{0:T(1024)S(1)} copy-done((s32[4096]{0:T(1024)S(1)}, s32[4096]{0:T(1024)}, u32[]{:S(2)}) %copy-start.4) | copy-done | bytes 16408
  5.5 0.0 copy-start.5
  5.5 0.7 %copy-done.5 = s32[4096]{0:T(1024)S(1)} copy-done((s32[4096]{0:T(1024)S(1)}, s32[4096]{0:T(1024)}, u32[]{:S(2)}) %copy-start.5) | copy-done | bytes 16408
  6.2 0.0 copy-start.7
  6.2 0.7 %copy-done.7 = f32[4,4,128]{2,1,0:T(4,128)S(1)} copy-done((f32[4,4,128]{2,1,0:T(4,128)S(1)}, f32[4,4,128]{2,1,0:T(4,128)}, u32[]{:S(2)}) %copy-start.7) | copy-done | bytes 8216
  6.9 51.4 %whole_kernel.1 = (f32[480,128]{1,0:T(8,128)S(1)}, f32[30,4096]{1,0:T(8,128)S(1)}) custom-call(f32[480,128]{1,0:T(8,128)S(1)} %bitcast.9, f32[16,128]{1,0:T(8,128)S(1)} %bitcast.14, f32[16,128]{1,0:T(8,128)S(1)} %bitcast.15, s32[32,128]{1,0:T(8,128)S(1)} %bitcast.10, f32[30,4096]{1,0:T(8,128)S(1)} %copy-done, f32[32,128]{1,0:T(8,128)S(1)} %bitcast.11, ...), custom_call_target="tpu_custom_call" | custom-call | tf_op jit(solution)/shard_map/whole_kernel/pallas_call | solution.py:356
  58.3 0.7 %copy.12 = f32[30,4,4,128]{3,2,1,0:T(4,128)} copy(f32[30,4,4,128]{3,2,1,0:T(4,128)S(1)} %bitcast.8) | data formatting | bytes 491520
  59.0 0.8 %copy.13 = f32[30,4096]{1,0:T(8,128)} copy(f32[30,4096]{1,0:T(8,128)S(1)} %get-tuple-element.9) | data formatting | bytes 983040
Async XLA Ops:
  0.6 0.7 %copy-start.6 = (f32[4,4,128]{2,1,0:T(4,128)S(1)}, f32[4,4,128]{2,1,0:T(4,128)}, u32[]{:S(2)}) copy-start(f32[4,4,128]{2,1,0:T(4,128)} %param.9) | copy-start | bytes 24580
  1.3 1.0 %copy-start = (f32[30,4096]{1,0:T(8,128)S(1)}, f32[30,4096]{1,0:T(8,128)}, u32[]{:S(2)}) copy-start(f32[30,4096]{1,0:T(8,128)} %compositions.1) | copy-start | bytes 1474564
  2.4 0.9 %copy-start.1 = (f32[30,4,4,128]{3,2,1,0:T(4,128)S(1)}, f32[30,4,4,128]{3,2,1,0:T(4,128)}, u32[]{:S(2)}) copy-start(f32[30,4,4,128]{3,2,1,0:T(4,128)} %param.8) | copy-start | bytes 737284
  3.3 0.7 %copy-start.2 = (s32[1,32,128]{2,1,0:T(8,128)S(1)}, s32[1,32,128]{2,1,0:T(8,128)}, u32[]{:S(2)}) copy-start(s32[1,32,128]{2,1,0:T(8,128)} %param.11) | copy-start | bytes 49156
  4.0 0.7 %copy-start.3 = (f32[4096]{0:T(1024)S(1)}, f32[4096]{0:T(1024)}, u32[]{:S(2)}) copy-start(f32[4096]{0:T(1024)} %param.13) | copy-start | bytes 49156
  4.8 0.7 %copy-start.4 = (s32[4096]{0:T(1024)S(1)}, s32[4096]{0:T(1024)}, u32[]{:S(2)}) copy-start(s32[4096]{0:T(1024)} %param.14) | copy-start | bytes 49156
  5.5 0.7 %copy-start.5 = (s32[4096]{0:T(1024)S(1)}, s32[4096]{0:T(1024)}, u32[]{:S(2)}) copy-start(s32[4096]{0:T(1024)} %param.15) | copy-start | bytes 49156
  6.2 0.7 %copy-start.7 = (f32[4,4,128]{2,1,0:T(4,128)S(1)}, f32[4,4,128]{2,1,0:T(4,128)}, u32[]{:S(2)}) copy-start(f32[4,4,128]{2,1,0:T(4,128)} %param.10) | copy-start | bytes 24580

commit v3 on v2

--- a/solution.py
+++ b/solution.py
@@ -11,6 +11,7 @@
 LANES = 128
 ROWS = 32
 GROUPS = ROWS // 8
+PLANE = 8
 F32 = jnp.float32
 BF16 = jnp.bfloat16
 
@@ -52,21 +53,22 @@
             fields[j] = mid + diffusion[j : j + 1, :] * (total - 6.0 * mid)
 
 
-def scatter_block(index, high, low, left, acc, groups):
-    width = index.shape[1]
-    group = (index >> 8).astype(F32).astype(BF16)
-    group = jnp.broadcast_to(group, (ROWS, width))
+def scatter_block(group, hot, high, low, left, acc, groups):
+    width = group.shape[1]
+    group = jnp.broadcast_to(group.astype(F32).astype(BF16), (ROWS, width))
     for g in range(groups):
         mask = group == jnp.array(g, BF16)
         zero = jnp.zeros((ROWS, width), BF16)
         left[2 * g * ROWS : (2 * g + 1) * ROWS, :] = jnp.where(mask, high, zero)
         left[(2 * g + 1) * ROWS : (2 * g + 2) * ROWS, :] = jnp.where(mask, low, zero)
-    place = lax.broadcasted_iota(jnp.int32, (256, width), 0)
-    right = jnp.where(place == (index & 255), 1.0, 0.0).astype(BF16)
-    part = lax.dot_general(
-        left[...], right, (((1,), (1,)), ((), ())), preferred_element_type=F32
+    acc[...] += lax.dot_general(
+        left[...], hot, (((1,), (1,)), ((), ())), preferred_element_type=F32
     )
-    acc[...] += part
+
+
+def hot_rows(index):
+    place = lax.broadcasted_iota(jnp.int32, (256, index.shape[1]), 0)
+    return jnp.where(place == (index & 255), 1.0, 0.0).astype(BF16)
 
 
 def acc_row(acc, j):
@@ -116,23 +118,33 @@
 
 
 def whole_kernel(
-    nx, ny, rows_x, rows_y,
-    means, diffusion, rate, lists, compositions, weights, slots, partners,
-    out, new,
-    cells, halo, fields, outgoing, received, local, moments, returned,
-    table, parts, pair, high, low, left1, acc1, left2, acc2,
-    halo_send, halo_recv, go_send, go_recv, back_send, back_recv,
+    nx, ny, rows_x, rows_y, *refs
 ):
+    inputs, (out, new_out), refs = refs[:8], refs[8:10], refs[10:]
+    staged, refs = refs[:8], refs[8:]
+    means, diffusion, rate, lists, compositions, weights, slots, partners = staged
+    (
+        new, cells, halo, fields, outgoing, received, local, moments, returned,
+        table, parts, pair, high, low, hot1, left1, acc1, left2, acc2,
+        in_sems, out_sem, halo_send, halo_recv, go_send, go_recv, back_send, back_recv,
+    ) = refs
     tiles = nx * ny
-    half = tiles // 2
+    planes = tiles // PLANE
     count = rows_x * rows_y
     species = compositions.shape[0]
     blocks = slots.shape[0]
     gx, gy = lax.axis_index("gx"), lax.axis_index("gy")
     me = gx * ny + gy
+    plane, inner = lax.div(me, PLANE), lax.rem(me, PLANE)
 
     def place(d):
         return (lax.div(d, ny), lax.rem(d, ny))
+
+    loads = [
+        pltpu.make_async_copy(inputs[i], staged[i], in_sems.at[i]) for i in range(8)
+    ]
+    for i in (0, 1, 2, 4, 7, 3, 6, 5):
+        loads[i].start()
 
     barrier = pltpu.get_barrier_semaphore()
 
@@ -145,6 +157,7 @@
 
     lax.fori_loop(1, tiles, greet, 0)
 
+    loads[0].wait()
     for x in range(rows_x):
         for y in range(rows_y):
             j = x * rows_y + y
@@ -181,7 +194,15 @@
         def _(i=i):
             halo[i] = jnp.zeros(halo.shape[1:], F32)
 
+    loads[4].wait()
+    loads[7].wait()
     gather_pairs(compositions, partners, table, parts, pair)
+    for i in (1, 2, 3, 5, 6):
+        loads[i].wait()
+    for b in range(0, blocks, 4):
+        index = jnp.concatenate([slots[b + i : b + i + 1, :] for i in range(4)], 1)
+        hot1[:, b * LANES : (b + 4) * LANES] = hot_rows(index)
+    local[...] = jnp.zeros(local.shape, F32)
 
     for i in range(4):
 
@@ -196,8 +217,8 @@
 
     def copy_of(buffers, sems, source, d, target):
         return pltpu.make_async_remote_copy(
-            src_ref=buffers[0].at[d],
-            dst_ref=buffers[1].at[source],
+            src_ref=buffers[0].at[d, 0 : species + 1],
+            dst_ref=buffers[1].at[source, 0 : species + 1],
             send_sem=sems[0].at[d],
             recv_sem=sems[1].at[source],
             device_id=place(target),
@@ -212,116 +233,107 @@
         for g in range(GROUPS):
             buffer[row, 8 * g : 8 * g + 8, :] = found[g]
 
-    def send_one(k):
-        d = lax.rem(me + k, tiles)
-        fill(d, outgoing, d)
-        copy_of(*go, me, d, d).start()
-
-    lax.fori_loop(0, half, lambda i, _: (send_one(half + i), 0)[1], 0)
-    lax.fori_loop(1, half, lambda i, _: (send_one(half - i), 0)[1], 0)
+    def send_plane(there, first):
+        def body(i, _):
+            d = there * PLANE + lax.rem(inner + i, PLANE)
+            fill(d, outgoing, d)
+            copy_of(*go, me, d, d).start()
+            return 0
+
+        lax.fori_loop(first, PLANE, body, 0)
+
+    def far_first(step):
+        half = planes // 2
+        lax.fori_loop(half, planes, lambda k, _: (step(k), 0)[1], 0)
+        lax.fori_loop(1, half, lambda k, _: (step(half - k), 0)[1], 0)
+
+    far_first(lambda k: send_plane(lax.rem(plane + k, planes), 0))
     fill(me, received, me)
-
-    def source_of(k):
-        return lax.rem(me + tiles - k, tiles)
-
-    def wait_for(which, k):
-        @pl.when(k > 0)
-        def _():
-            s = source_of(k)
+    send_plane(plane, 1)
+
+    def wait_plane(which, there, first):
+        def body(i, _):
+            s = there * PLANE + lax.rem(inner + i, PLANE)
             copy_of(*which, s, s, s).wait_recv()
-
-    step_of = 8
-
-    def arrivals(first_k, sign):
-        def batch(n, _):
-            ks = [first_k + sign * (n * step_of + i) for i in range(step_of)]
-            for k in ks:
-                wait_for(go, k)
-
-            def body(b, _):
-                index = slots[pl.ds(b, 1), :]
-                lane = jnp.broadcast_to(index & (LANES - 1), (8, LANES))
-                chunk = jnp.broadcast_to(index >> 7, (8, LANES))
-                sums = [local[b, 8 * g : 8 * g + 8, :] for g in range(GROUPS)]
-                for k in ks:
-                    s = source_of(k)
-                    mask = chunk == s
-                    for g in range(GROUPS):
-                        rows = received[s, 8 * g : 8 * g + 8, :]
-                        found = jnp.take_along_axis(
-                            rows, lane, axis=1, mode="promise_in_bounds"
-                        )
-                        sums[g] = jnp.where(mask, found, sums[g])
+            return 0
+
+        lax.fori_loop(first, PLANE, body, 0)
+
+    per = left1.shape[1]
+
+    def work(there, first):
+        wait_plane(go, there, first)
+
+        def body(b, _):
+            index = slots[pl.ds(b, 1), :]
+            lane = jnp.broadcast_to(index & (LANES - 1), (8, LANES))
+            chunk = jnp.broadcast_to((index >> 7) - there * PLANE, (8, LANES))
+            sums = [local[b, 8 * g : 8 * g + 8, :] for g in range(GROUPS)]
+            for i in range(PLANE):
+                mask = chunk == i
                 for g in range(GROUPS):
-                    local[b, 8 * g : 8 * g + 8, :] = sums[g]
-                return 0
-
-            lax.fori_loop(0, blocks, body, 0, unroll=2)
+                    rows = received[there * PLANE + i, 8 * g : 8 * g + 8, :]
+                    found = jnp.take_along_axis(rows, lane, axis=1, mode="promise_in_bounds")
+                    sums[g] = jnp.where(mask, found, sums[g])
+            for g in range(GROUPS):
+                local[b, 8 * g : 8 * g + 8, :] = sums[g]
+            at = pl.multiple_of(b * LANES, LANES)
+            cell = jnp.concatenate(sums, 0)
+            mine = compositions[:, pl.ds(at, LANES)]
+            fresh = mine - cell[species : species + 1, :] * (mine - cell[:species, :])
+            fresh = fresh - pair[0:species, pl.ds(at, LANES)]
+            new[:, pl.ds(at, LANES)] = fresh
+            weight = weights[pl.ds(b, 1), :]
+            values = jnp.concatenate(
+                [weight * fresh, weight, jnp.zeros((ROWS - species - 1, LANES), F32)], 0
+            )
+            top = values.astype(BF16)
+            high[:, pl.ds(at, LANES)] = top
+            low[:, pl.ds(at, LANES)] = (values - top.astype(F32)).astype(BF16)
             return 0
 
-        lax.fori_loop(0, half // step_of, batch, 0)
-
-    local[...] = jnp.zeros(local.shape, F32)
-    arrivals(half, 1)
-    arrivals(half - 1, -1)
-
-    def mix(b, _):
-        at = pl.multiple_of(b * LANES, LANES)
-        mine = compositions[:, pl.ds(at, LANES)]
-        fresh = mine - local[b, species : species + 1, :] * (mine - local[b, 0:species, :])
-        fresh = fresh - pair[0:species, pl.ds(at, LANES)]
-        new[:, pl.ds(at, LANES)] = fresh
-        weight = weights[pl.ds(b, 1), :]
-        values = jnp.concatenate(
-            [weight * fresh, weight, jnp.zeros((ROWS - species - 1, LANES), F32)], 0
-        )
-        first = values.astype(BF16)
-        high[:, pl.ds(at, LANES)] = first
-        low[:, pl.ds(at, LANES)] = (values - first.astype(F32)).astype(BF16)
-        return 0
-
-    lax.fori_loop(0, blocks, mix, 0, unroll=2)
-    acc1[...] = jnp.zeros(acc1.shape, F32)
-    per = left1.shape[1] // LANES
-
-    def gather_moments(k, _):
-        index = jnp.concatenate([slots[pl.ds(k * per + i, 1), :] for i in range(per)], 1)
-        at = pl.multiple_of(k * per * LANES, per * LANES)
-        cols = pl.ds(at, per * LANES)
-        scatter_block(index, high[:, cols], low[:, cols], left1, acc1, half)
-        return 0
-
-    lax.fori_loop(0, blocks // per, gather_moments, 0)
-    for s in range(tiles):
-        moments[s] = acc_row(acc1, s)
-
-    def return_one(k):
-        d = lax.rem(me + k, tiles)
-        copy_of(*back, me, d, d).start()
-
-    lax.fori_loop(0, half, lambda i, _: (return_one(half + i), 0)[1], 0)
-    lax.fori_loop(1, half, lambda i, _: (return_one(half - i), 0)[1], 0)
+        lax.fori_loop(0, blocks, body, 0, unroll=2)
+        acc1[...] = jnp.zeros(acc1.shape, F32)
+
+        def scatter(k, _):
+            rows = [slots[pl.ds(k * (per // LANES) + i, 1), :] for i in range(per // LANES)]
+            group = (jnp.concatenate(rows, 1) >> 8) - there * (PLANE // 2)
+            cols = pl.ds(pl.multiple_of(k * per, per), per)
+            scatter_block(
+                group, hot1[:, cols], high[:, cols], low[:, cols], left1, acc1, PLANE // 2
+            )
+            return 0
+
+        lax.fori_loop(0, blocks * LANES // per, scatter, 0)
+        for i in range(PLANE):
+            moments[there * PLANE + i] = acc_row(acc1, i)
+
+        def body_back(i, _):
+            d = there * PLANE + lax.rem(inner + i, PLANE)
+            copy_of(*back, me, d, d).start()
+            return 0
+
+        lax.fori_loop(first, PLANE, body_back, 0)
+
+    far_first(lambda k: work(lax.rem(plane + planes - k, planes), 0))
+    work(plane, 1)
+    store = pltpu.make_async_copy(new, new_out, out_sem)
+    store.start()
     returned[me] = moments[me]
 
     acc2[...] = jnp.zeros(acc2.shape, F32)
-    per2 = left2.shape[1] // LANES
-
-    def returns(first_k, sign):
-        def batch(n, _):
-            ks = [first_k + sign * (n * per2 + i) for i in range(per2)]
-            for k in ks:
-                wait_for(back, k)
-            values = jnp.concatenate([returned[source_of(k)] for k in ks], 1)
-            index = jnp.concatenate([lists[pl.ds(source_of(k), 1), :] for k in ks], 1)
-            first = values.astype(BF16)
-            second = (values - first.astype(F32)).astype(BF16)
-            scatter_block(index, first, second, left2, acc2, count // 2)
-            return 0
-
-        lax.fori_loop(0, half // per2, batch, 0)
-
-    returns(half, 1)
-    returns(half - 1, -1)
+
+    def collect(there, first):
+        wait_plane(back, there, first)
+        at = [there * PLANE + i for i in range(PLANE)]
+        values = jnp.concatenate([returned[s] for s in at], 1)
+        index = jnp.concatenate([lists[pl.ds(s, 1), :] for s in at], 1)
+        top = values.astype(BF16)
+        rest = (values - top.astype(F32)).astype(BF16)
+        scatter_block(index >> 8, hot_rows(index), top, rest, left2, acc2, count // 2)
+
+    far_first(lambda k: collect(lax.rem(plane + k, planes), 0))
+    collect(plane, 1)
     for j in range(count):
         total = acc_row(acc2, j)
         mean = (total[:species] + fields[j, 0:species, :]) / (total[species : species + 1] + 1.0)
@@ -340,6 +352,7 @@
         return 0
 
     lax.fori_loop(1, tiles, finish, 0)
+    store.wait()
 
 
 def on_device(
@@ -350,9 +363,18 @@
     tiles = send_lists.shape[1]
     particles = compositions.shape[1]
     blocks = particles // LANES
-    width = 512
     vmem = lambda *shape: pltpu.VMEM(shape, F32)
     half_vmem = lambda *shape: pltpu.VMEM(shape, BF16)
+    operands = (
+        cell_means.reshape(species * count, depth),
+        diffusion.reshape(count, depth),
+        mix_rate.reshape(count, depth),
+        send_lists[0],
+        compositions,
+        weights.reshape(blocks, LANES),
+        particle_slots.reshape(blocks, LANES),
+        partners.reshape(blocks, LANES),
+    )
     out, new = pl.pallas_call(
         functools.partial(
             whole_kernel, lax.axis_size("gx"), lax.axis_size("gy"), rows_x, rows_y
@@ -361,10 +383,15 @@
             jax.ShapeDtypeStruct((species * count, LANES), F32),
             jax.ShapeDtypeStruct((species, particles), F32),
         ),
-        in_specs=[pl.BlockSpec(memory_space=pltpu.VMEM)] * 8,
-        out_specs=[pl.BlockSpec(memory_space=pltpu.VMEM)] * 2,
+        in_specs=[pl.BlockSpec(memory_space=pltpu.HBM)] * 8,
+        out_specs=[
+            pl.BlockSpec(memory_space=pltpu.VMEM),
+            pl.BlockSpec(memory_space=pltpu.HBM),
+        ],
         name="whole_kernel",
-        scratch_shapes=[
+        scratch_shapes=[pltpu.VMEM(a.shape, a.dtype) for a in operands]
+        + [
+            vmem(species, particles),
             vmem(rows_x, rows_y, ROWS, LANES),
             vmem(4, max(rows_x, rows_y), ROWS, LANES),
             vmem(count, ROWS, LANES),
@@ -378,10 +405,13 @@
             vmem(ROWS, particles),
             half_vmem(ROWS, particles),
             half_vmem(ROWS, particles),
-            half_vmem(tiles * ROWS, width),
-            vmem(tiles * ROWS, 256),
-            half_vmem(count * ROWS, width),
+            half_vmem(256, particles),
+            half_vmem(PLANE * ROWS, 1024),
+            vmem(PLANE * ROWS, 256),
+            half_vmem(count * ROWS, PLANE * LANES),
             vmem(count * ROWS, 256),
+            pltpu.SemaphoreType.DMA((8,)),
+            pltpu.SemaphoreType.DMA,
             pltpu.SemaphoreType.DMA((4,)),
             pltpu.SemaphoreType.DMA((4,)),
             pltpu.SemaphoreType.DMA((tiles,)),
@@ -390,18 +420,9 @@
             pltpu.SemaphoreType.DMA((tiles,)),
         ],
         compiler_params=pltpu.CompilerParams(
-            collective_id=0, has_side_effects=True, vmem_limit_bytes=44 * 1024 * 1024
+            collective_id=0, has_side_effects=True, vmem_limit_bytes=63 * 1024 * 1024
         ),
-    )(
-        cell_means.reshape(species * count, depth),
-        diffusion.reshape(count, depth),
-        mix_rate.reshape(count, depth),
-        send_lists[0],
-        compositions,
-        weights.reshape(blocks, LANES),
-        particle_slots.reshape(blocks, LANES),
-        partners.reshape(blocks, LANES),
-    )
+    )(*operands)
     return out.reshape(species, rows_x, rows_y, depth), new
 
 

time: 60.4 us -> 48.4 us (0.80)
  Pallas kernels: 51.4 us -> 44 us
  local copies, waits for them, and re-layouts: 7.73 us -> 3.52 us
    pallas_call x1, Pallas kernels: 51.4 us -> 44 us  [on_device(): pl.pallas_call(functools.partial(whole_kernel, lax.axis_size('gx'), lax.a...]
    unnamed x18 -> x2, local copies, waits for them, and re-layouts: 7.73 us -> 3.52 us
where the time goes in v3:
time: 48.4 us; the launch traced here: 48.2 us
  Pallas kernels  44 us (91%)
  local copies, waits for them, and re-layouts  3.52 us (7%)
  between operations  0.64 us (1%)
    pallas_call x1, Pallas kernels, on_device(): pl.pallas_call(functools.partial(whole_kernel, lax.axis_size('gx'), lax.a...  44 us
    unnamed x2, local copies, waits for them, and re-layouts  3.52 us

profile of v3, /device:TPU:0, one launch (start us, length us, event | category | flops | bytes accessed | tf_op | source)
XLA Modules:
  0.0 48.2 jit_solution(3247796173494330800)
XLA Ops:
  0.6 44.0 %whole_kernel.1 = (f32[480,128]{1,0:T(8,128)}, f32[30,4096]{1,0:T(8,128)}) custom-call(f32[480,128]{1,0:T(8,128)} %bitcast.9, f32[16,128]{1,0:T(8,128)} %bitcast.14, f32[16,128]{1,0:T(8,128)} %bitcast.15, s32[32,128]{1,0:T(8,128)} %bitcast.10, f32[30,4096]{1,0:T(8,128)} %refs_4_.1, f32[32,128]{1,0:T(8,128)} %bitcast.11, s32[32,128]{1,0:T(8,128)} %bitcast.12, ...), custom_call_target="tpu_custom_call" | custom-call | tf_op jit(solution)/shard_map/whole_kernel/pallas_call | solution.py:378
  44.7 1.7 %copy.12 = f32[30,4,4,128]{3,2,1,0:T(4,128)} copy(f32[30,4,4,128]{3,2,1,0:T(4,128)} %bitcast.8) | data formatting | bytes 491520
  46.3 1.9 %copy.13 = f32[30,4096]{1,0:T(8,128)} copy(f32[30,4096]{1,0:T(8,128)} %get-tuple-element.9) | data formatting | bytes 983040

commit v4 on v3

--- a/solution.py
+++ b/solution.py
@@ -292,7 +292,7 @@
             low[:, pl.ds(at, LANES)] = (values - top.astype(F32)).astype(BF16)
             return 0
 
-        lax.fori_loop(0, blocks, body, 0, unroll=2)
+        lax.fori_loop(0, blocks, body, 0, unroll=4)
         acc1[...] = jnp.zeros(acc1.shape, F32)
 
         def scatter(k, _):
@@ -353,6 +353,11 @@
 
     lax.fori_loop(1, tiles, finish, 0)
     store.wait()
+
+
+def hand_over(first, second, first_out, second_out):
+    first_out[...] = first[...]
+    second_out[...] = second[...]
 
 
 def on_device(
@@ -423,6 +428,13 @@
             collective_id=0, has_side_effects=True, vmem_limit_bytes=63 * 1024 * 1024
         ),
     )(*operands)
+    out, new = pl.pallas_call(
+        hand_over,
+        out_shape=tuple(jax.ShapeDtypeStruct(a.shape, a.dtype) for a in (out, new)),
+        in_specs=[pl.BlockSpec(memory_space=pltpu.VMEM)] * 2,
+        out_specs=[pl.BlockSpec(memory_space=pltpu.VMEM)] * 2,
+        name="hand_over",
+    )(out, new)
     return out.reshape(species, rows_x, rows_y, depth), new
 
 

time: 48.4 us -> 45.6 us (0.942)
  local copies, waits for them, and re-layouts: 3.52 us -> 0 us
  Pallas kernels: 44 us -> 44.8 us
    unnamed x2 -> x0, local copies, waits for them, and re-layouts: 3.52 us -> none
    pallas_call x0 -> x1, Pallas kernels: none -> 2.07 us  [on_device(): pl.pallas_call(hand_over, out_shape=tuple((jax.ShapeDtypeStruct(a.shape,...]
    pallas_call x1, Pallas kernels: 44 us -> 42.7 us  [on_device(): pl.pallas_call(functools.partial(whole_kernel, lax.axis_size('gx'), lax.a...]
where the time goes in v4:
time: 45.6 us; the launch traced here: 45.5 us
  Pallas kernels  44.8 us (98%)
  between operations  0.64 us (1%)
    pallas_call x1, Pallas kernels, on_device(): pl.pallas_call(functools.partial(whole_kernel, lax.axis_size('gx'), lax.a...  42.7 us
    pallas_call x1, Pallas kernels, on_device(): pl.pallas_call(hand_over, out_shape=tuple((jax.ShapeDtypeStruct(a.shape,...  2.07 us

profile of v4, /device:TPU:0, one launch (start us, length us, event | category | flops | bytes accessed | tf_op | source)
XLA Modules:
  0.0 45.5 jit_solution(13292623344557346579)
XLA Ops:
  0.6 42.7 %whole_kernel.1 = (f32[480,128]{1,0:T(8,128)}, f32[30,4096]{1,0:T(8,128)}) custom-call(f32[480,128]{1,0:T(8,128)} %bitcast.8, f32[16,128]{1,0:T(8,128)} %bitcast.13, f32[16,128]{1,0:T(8,128)} %bitcast.14, s32[32,128]{1,0:T(8,128)} %bitcast.9, f32[30,4096]{1,0:T(8,128)} %refs_4_.1, f32[32,128]{1,0:T(8,128)} %bitcast.10, s32[32,128]{1,0:T(8,128)} %bitcast.11, ...), custom_call_target="tpu_custom_call" | custom-call | tf_op jit(solution)/shard_map/whole_kernel/pallas_call | solution.py:383
  43.4 2.1 %hand_over.1 = (f32[480,128]{1,0:T(8,128)}, f32[30,4096]{1,0:T(8,128)}) custom-call(f32[480,128]{1,0:T(8,128)} %get-tuple-element.6.first, f32[30,4096]{1,0:T(8,128)} %get-tuple-element.7.second), custom_call_target="tpu_custom_call" | custom-call | tf_op jit(solution)/shard_map/hand_over/pallas_call | solution.py:431
